TPU v7x, 256 devices: a whole 4x4x8 slice. The times are simulated.
256 devices in a mesh: blk: 32 (over z, y_lo, core), group: 8 (over x, y_hi).
Axes of the slice: x: 4, y: 4 (y_hi: 2, y_lo: 2; y = y_hi * 2 + y_lo), z: 8, core: 2. Of those that a mesh axis runs over, the one named last changes fastest.
Arguments:
- image_embed: bfloat16 [32768, 1152], P(('group', 'blk')), parts along dimension 0, may hold values from -0.5 to 0.5
- text_embed: bfloat16 [32768, 1152], P(('group', 'blk')), parts along dimension 0, may hold values from -0.5 to 0.5
- logit_scale: float32 [1], replicated, may hold values from 4 to 12
- logit_bias: float32 [1], replicated, may hold values from -4 to -1
Outputs:
- row_loss: float32 [32768], P(('group', 'blk')), parts along dimension 0
- image_grad: float32 [32768, 1152], P(('group', 'blk')), parts along dimension 0
- text_grad: float32 [32768, 1152], P(('group', 'blk')), parts along dimension 0
There are 8 independent parts, one for each index of `group`. A program takes and returns all parts, laid end to end along the dimension named above; an argument that names none is the same for every part. Nothing has to cross between parts.
All inputs are finite; a program needn't handle non-finite values.
Results may differ from a plain program's by a relative error of at most 0.0085.
Values may be sent and summed in bfloat16 or wider, within the bound.
A program may use at most 128 MiB of HBM per device.

v0:
```python
import functools

import jax
import jax.numpy as jnp
from jax import lax
from jax.experimental import pallas as pl
from jax.experimental.pallas import tpu as pltpu
from jax.sharding import PartitionSpec as P

MESH = pl.DeviceIdType.MESH
F32 = jnp.float32
BF16 = jnp.bfloat16

RING = 8
QUAD = 4
RIGHT, LEFT = 0, 1
LATE, EARLY = 0, 1
EPS = 1e-06
CODE = 2.0**13
TINY = 2.0**-126


def encode(x):
    a = x * CODE
    a2 = a * a
    return (a2 * a2 * a).astype(BF16)


def decode(y):
    y = y.astype(F32)
    root = jnp.exp(jnp.log(jnp.maximum(jnp.abs(y), TINY)) * 0.2) * (1.0 / CODE)
    return jnp.where(y < 0, -root, root)


def nt(a, b):
    return lax.dot_general(a, b, (((1,), (1,)), ((), ())), preferred_element_type=F32)


def tn(a, b):
    return lax.dot_general(a, b, (((0,), (0,)), ((), ())), preferred_element_type=F32)


def unnormal(g, u, inv, scale):
    along = jnp.sum(u * g, axis=1, keepdims=True)
    return (g - u * along) * (inv[:, 0:1] * scale)


def kernel(
    img_hbm,
    txt_hbm,
    both_ref,
    loss_ref,
    gi_ref,
    gt_ref,
    late_ref,
    unit_i,
    inv_i,
    img_ref,
    txt_ref,
    img,
    txt,
    part,
    coefs,
    sums,
    rs_send,
    rs_recv,
    core_recv,
    y_send,
    y_recv,
    unit_t,
    inv_t,
    loss_part,
    loss_send,
    loss_recv,
    in_sem,
    ag_ssem,
    ag_rsem,
    rs_ssem,
    rs_rsem,
    loss_ssem,
    loss_rsem,
    t_ssem,
    t_rsem,
    c_ssem,
    c_rsem,
    y_ssem,
    y_rsem,
):
    rows = img_ref.shape[0]
    half = rows // 2
    sub = half // 2
    me = lax.axis_index("blk")
    n = RING * QUAD
    to = (lax.rem(me + QUAD, n), lax.rem(me + n - QUAD, n))
    other_core = me + 1 - 2 * lax.rem(me, 2)
    other_y = me + 2 - 4 * lax.rem(lax.div(me, 2), 2)

    def copy(src, dst, ssem, rsem, device):
        return pltpu.make_async_remote_copy(
            src_ref=src,
            dst_ref=dst,
            send_sem=ssem,
            recv_sem=rsem,
            device_id={"blk": device},
            device_id_type=MESH,
        )

    barrier = pltpu.get_barrier_semaphore()
    for peer in (*to, other_core, other_y):
        pl.semaphore_signal(barrier, inc=1, device_id={"blk": peer}, device_id_type=MESH)

    def load(i):
        src, dst = ((img_hbm, img_ref), (txt_hbm, txt_ref))[i // 2]
        some = pl.ds(i % 2 * half, half)
        return pltpu.make_async_copy(src.at[some, :], dst.at[some, :], in_sem.at[i])

    for i in range(4):
        load(i).start()

    def normalize(src, at, size, unit, inv, out):
        values = src[pl.ds(at, size), :].astype(F32)
        norm = jnp.sqrt(jnp.sum(values * values, axis=1, keepdims=True) + EPS)
        inverse = 1.0 / norm
        u = values * inverse
        unit[pl.ds(at, size), :] = u
        inv[pl.ds(at, size), :] = jnp.broadcast_to(inverse, (size, 128))
        out[pl.ds(at, size), :] = u.astype(BF16)

    def place(way, i, s):
        side = way if i < 6 else 1 - way
        return s * half + side * sub

    def gather(way, i, s):
        if i < 2:
            piece = i if way == RIGHT else 1 - i
            src = img.at[0, pl.ds(piece * half + s * sub, sub), :]
        else:
            src = img.at[i - 1, pl.ds(place(way, i - 2, s), sub), :]
        dst = img.at[i + 1, pl.ds(place(way, i, s), sub), :]
        return copy(src, dst, ag_ssem.at[way, i, s], ag_rsem.at[way, i, s], to[way])

    for i in range(2):
        load(i).wait()
        normalize(img_ref, i * half, half, unit_i, inv_i, img.at[0])
        if i == 0:
            pl.semaphore_wait(barrier, 4)
        for s in range(2):
            gather(i, 0, s).start()
    for s in range(2):
        for way in (RIGHT, LEFT):
            gather(way, 1, s).start()

    for i in range(2):
        load(2 + i).wait()
        normalize(txt_ref, i * half, half, unit_t, inv_t, txt)

    scale = both_ref[0:1, 0:1]
    bias = both_ref[1:2, 0:1]

    def text_copy(i):
        src = (0, 0, 2)[i]
        dst = (1, 2, 3)[i]
        device = (other_core, other_y, other_core)[i]
        return copy(
            txt.at[pl.ds(src * rows, rows), :],
            txt.at[pl.ds(dst * rows, rows), :],
            t_ssem.at[i],
            t_rsem.at[i],
            device,
        )

    text_copy(1).start()
    text_copy(0).start()

    def tile(block, at, size, maybe_own=False):
        some = pl.ds(at, size)
        wide = 2 * rows
        total = jnp.zeros((size, rows), F32)
        for h in range(2):
            m = nt(img[block, some, :], txt[pl.ds(h * wide, wide), :]) * scale + bias
            if maybe_own and h == 0:
                row = lax.broadcasted_iota(jnp.int32, m.shape, 0)
                col = lax.broadcasted_iota(jnp.int32, m.shape, 1)
                eye = row + jnp.where(block == 0, 0, 2 * wide) == col
                m = jnp.where(eye, -m, m)
            e = jnp.exp(-jnp.abs(m))
            soft = jnp.maximum(m, 0.0) + jnp.log1p(e)
            r = 1.0 / (1.0 + e)
            coef = jnp.where(m >= 0, r, e * r)
            if maybe_own and h == 0:
                coef = jnp.where(eye, -coef, coef)
            total = total + soft[:, :rows] + soft[:, rows:]
            coefs[block, some, pl.ds(h * wide, wide)] = coef.astype(BF16)
        part[block, some, :] = jnp.dot(
            coefs[block, some, :], txt[...], preferred_element_type=F32
        )
        if size < rows:
            total = jnp.concatenate([total, total], axis=0)
        across = jnp.sum(total.T, axis=0, keepdims=True)
        if size < rows:
            lane = lax.broadcasted_iota(jnp.int32, (1, rows), 1)
            across = jnp.where(lane < at, loss_part[block], across)
        loss_part[block] = across

    def serve(i, s):
        for way in (RIGHT, LEFT):
            gather(way, i, s).wait_recv()
            if i < 5:
                gather(way, i + 2, s).start()

    def gather_wait(way, i, s):
        row = pl.multiple_of(place(way, i, s), sub)
        some = img.at[i + 1, pl.ds(row, sub), :]
        copy(some, some, ag_ssem.at[way, i, s], ag_rsem.at[way, i, s], to[way]).wait_recv()

    def block_of(kind, j):
        return (7, 6, 4, 2)[j] if kind == LATE else (5, 3, 1)[j]

    def chunk(way, kind, j, s):
        at = 4 * kind + j
        some = pl.ds(pl.multiple_of(s * sub, sub), sub)
        very_last = kind == LATE and j == 3 and s == 1
        return copy(
            rs_send.at[way, at, some, :],
            late_ref.at[way] if very_last else rs_recv.at[way, at, some, :],
            rs_ssem.at[way, at, s],
            rs_rsem.at[way, at, s],
            to[way],
        )

    def pass_on(kind, j, first=0, count=2):
        def one(s, _):
            some = pl.ds(pl.multiple_of(s * sub, sub), sub)
            for way in (RIGHT, LEFT):
                row = pl.multiple_of(s * half + (1 - way) * sub, sub)
                x = part[block_of(kind, j), pl.ds(row, sub), :]
                if j > 0:
                    chunk(way, kind, j - 1, s).wait_recv()
                    x = x + decode(rs_recv[way, 4 * kind + j - 1, some, :])
                rs_send[way, 4 * kind + j, some, :] = encode(x)
                chunk(way, kind, j, s).start()
            return 0

        if j == 3:
            one(0, 0)
            one(1, 0)
        else:
            lax.fori_loop(first, first + count, one, 0)

    def loss_copy(way, kind, j):
        at = 4 * kind + j
        return copy(
            loss_send.at[way, at],
            loss_recv.at[way, at],
            loss_ssem.at[way, at],
            loss_rsem.at[way, at],
            to[way],
        )

    def loss_on(kind, j):
        for way in (RIGHT, LEFT):
            x = loss_part[block_of(kind, j)]
            if j > 0:
                loss_copy(way, kind, j - 1).wait_recv()
                x = x + loss_recv[way, 4 * kind + j - 1]
            loss_send[way, 4 * kind + j] = x
            loss_copy(way, kind, j).start()

    for i in range(2):
        serve(i, 0)
        serve(i, 1)
    text_copy(1).wait_recv()
    text_copy(2).start()
    serve(2, 0)
    serve(2, 1)
    text_copy(0).wait_recv()
    text_copy(2).wait_recv()

    def work(k, _):
        @pl.when(k == 1)
        def _():
            serve(3, 0)

        @pl.when(k == 2)
        def _():
            serve(3, 1)

        @pl.when(k == 4)
        def _():
            serve(4, 0)
            serve(4, 1)

        @pl.when(k == 5)
        def _():
            loss_on(EARLY, 0)
            pass_on(EARLY, 0)

        @pl.when(k == 6)
        def _():
            serve(5, 0)
            serve(5, 1)

        tile(jnp.where(k < 5, k + 1, jnp.where(k == 5, 0, 6)), 0, rows, True)
        return 0

    lax.fori_loop(0, 7, work, 0)

    def farthest(s, _):
        for way in (RIGHT, LEFT):
            gather_wait(way, 6, s)
        tile(7, pl.multiple_of(s * half, half), half)
        pl.when(s == 1)(lambda: loss_on(LATE, 0))
        pass_on(LATE, 0, s, 1)
        return 0

    lax.fori_loop(0, 2, farthest, 0)

    def text_sums(b):
        sums[b] = tn(
            coefs[:, :, pl.ds(pl.multiple_of(b * rows, rows), rows)].reshape(RING * rows, rows),
            img[...].reshape(RING * rows, img.shape[2]),
        )

    def core_copy(i):
        return copy(sums.at[1 + 2 * i], core_recv.at[i], c_ssem.at[i], c_rsem.at[i], other_core)

    y_copy = copy(y_send, y_recv, y_ssem.at[0], y_rsem.at[0], other_y)

    def sums_work(k, _):
        b = jnp.where(k == 0, 3, jnp.where(k == 1, 1, jnp.where(k == 2, 2, 0)))
        text_sums(b)

        @pl.when(k == 0)
        def _():
            core_copy(1).start()

        @pl.when(k == 1)
        def _():
            core_copy(0).start()
            loss_on(EARLY, 1)
            pass_on(EARLY, 1)

        return 0

    lax.fori_loop(0, QUAD, sums_work, 0)
    loss_on(LATE, 1)
    pass_on(LATE, 1)
    core_copy(1).wait_recv()
    y_send[...] = encode(sums[2] + core_recv[1])
    y_copy.start()
    loss_on(EARLY, 2)
    pass_on(EARLY, 2, 0, 1)
    loss_on(LATE, 2)
    pass_on(LATE, 2)
    pass_on(EARLY, 2, 1, 1)
    core_copy(0).wait_recv()
    sums[0] += core_recv[0]
    loss_on(LATE, 3)
    pass_on(LATE, 3)

    def sent(i, _):
        for way in (RIGHT, LEFT):
            for s in range(2):
                some = img.at[i, pl.ds(s * sub, sub), :]
                copy(some, some, ag_ssem.at[way, i, s], ag_rsem.at[way, i, s], to[way]).wait_send()
        return 0

    lax.fori_loop(0, 7, sent, 0)
    for i in range(3):
        text_copy(i).wait_send()
    for i in range(2):
        core_copy(i).wait_send()

    def summed(at):
        for way in (RIGHT, LEFT):
            for s in range(2):
                some = rs_send.at[way, at, pl.ds(s * sub, sub), :]
                copy(some, some, rs_ssem.at[way, at, s], rs_rsem.at[way, at, s], to[way]).wait_send()
            x = loss_send.at[way, at]
            copy(x, x, loss_ssem.at[way, at], loss_rsem.at[way, at], to[way]).wait_send()

    lax.fori_loop(0, 3, lambda i, _: (summed(i), 0)[1], 0)
    lax.fori_loop(4, 7, lambda i, _: (summed(i), 0)[1], 0)

    def own_rows(way, kind, s):
        at = (half if (way == RIGHT) == (kind == EARLY) else 0) + s * sub
        return pl.ds(pl.multiple_of(at, sub), sub)

    def last(way, kind, s):
        some = pl.ds(pl.multiple_of(s * sub, sub), sub)
        chunk(way, kind, 3 - kind, s).wait_recv()
        at = own_rows(way, kind, s)
        return at, part[0, at, :] + decode(rs_recv[way, 4 * kind + 3 - kind, some, :])

    def add_early(s, _):
        for way in (RIGHT, LEFT):
            at, x = last(way, EARLY, s)
            part[0, at, :] = x
        return 0

    lax.fori_loop(0, 2, add_early, 0)
    y_copy.wait_recv()

    def finish_text(i, _):
        at = pl.ds(pl.multiple_of(i * sub, sub), sub)
        g = sums[0, at, :] + decode(y_recv[at, :])
        gt_ref[at, :] = unnormal(g, unit_t[at, :], inv_t[at, :], scale)
        return 0

    lax.fori_loop(0, 4, finish_text, 0)

    def lanes(way, kind):
        loss_copy(way, kind, 3 - kind).wait_recv()
        x = loss_recv[way, 4 * kind + 3 - kind]
        at = (1 - way) * sub
        return [x[:, s * half + at : s * half + at + sub] for s in range(2)]

    loss_ref[...] = (
        loss_part[0]
        + jnp.concatenate(lanes(RIGHT, LATE) + lanes(RIGHT, EARLY), axis=1)
        + jnp.concatenate(lanes(LEFT, EARLY) + lanes(LEFT, LATE), axis=1)
    )
    y_copy.wait_send()

    for way in (RIGHT, LEFT):
        at = own_rows(way, LATE, 1)
        gi_ref[at, :] = part[0, at, :]
    for way in (RIGHT, LEFT):
        at, g = last(way, LATE, 0)
        gi_ref[at, :] = unnormal(g, unit_i[at, :], inv_i[at, :], scale)
    for way in (RIGHT, LEFT):
        chunk(way, LATE, 3, 1).wait_recv()
    summed(3)


def write_out(
    loss_in, gi_in, gt_in, late, unit, inv, both, loss_out, gi_out, gt_out, row, rest, sem
):
    sub = late.shape[1]
    row[...] = loss_in[0]
    copies = [
        pltpu.make_async_copy(gt_in, gt_out, sem.at[0]),
        pltpu.make_async_copy(row, loss_out, sem.at[1]),
    ]
    for way in (RIGHT, LEFT):
        some = pl.ds(way * 2 * sub, sub)
        copies.append(pltpu.make_async_copy(gi_in.at[some, :], gi_out.at[some, :], sem.at[2 + way]))
    for c in copies:
        c.start()
    scale = both[0:1, 0:1]
    for way in (RIGHT, LEFT):
        some = pl.ds(way * 2 * sub + sub, sub)
        g = gi_in[some, :] + decode(late[way])
        rest[way] = unnormal(g, unit[some, :], inv[some, :], scale)
        c = pltpu.make_async_copy(rest.at[way], gi_out.at[some, :], sem.at[4 + way])
        c.start()
        copies.append(c)
    for c in copies:
        c.wait()


def per_device(image_embed, text_embed, logit_scale, logit_bias):
    rows, width = image_embed.shape
    half = rows // 2
    dma = pltpu.SemaphoreType.DMA
    vmem = pl.BlockSpec(memory_space=pltpu.VMEM)
    hbm = pl.BlockSpec(memory_space=pltpu.HBM)
    image_embed = pltpu.with_memory_space_constraint(image_embed, pltpu.HBM)
    text_embed = pltpu.with_memory_space_constraint(text_embed, pltpu.HBM)
    row = lax.broadcasted_iota(jnp.int32, (8, 128), 0)
    both = jnp.where(row == 0, logit_scale[0], logit_bias[0])
    anywhere = pl.BlockSpec(memory_space=pl.ANY)
    results = pl.pallas_call(
        kernel,
        out_shape=(
            pltpu.VMEM((1, rows), F32),
            pltpu.VMEM((rows, width), F32),
            pltpu.VMEM((rows, width), F32),
            pltpu.VMEM((2, rows // 4, width), BF16),
            pltpu.VMEM((rows, width), F32),
            pltpu.VMEM((rows, 128), F32),
        ),
        in_specs=[hbm, hbm, vmem],
        out_specs=(vmem,) * 6,
        scratch_shapes=[
            pltpu.VMEM((rows, width), BF16),
            pltpu.VMEM((rows, width), BF16),
            pltpu.VMEM((RING, rows, width), BF16),
            pltpu.VMEM((QUAD * rows, width), BF16),
            pltpu.VMEM((RING, rows, width), F32),
            pltpu.VMEM((RING, rows, QUAD * rows), BF16),
            pltpu.VMEM((QUAD, rows, width), F32),
            pltpu.VMEM((2, 7, half, width), BF16),
            pltpu.VMEM((2, 7, half, width), BF16),
            pltpu.VMEM((2, rows, width), F32),
            pltpu.VMEM((rows, width), BF16),
            pltpu.VMEM((rows, width), BF16),
            pltpu.VMEM((rows, width), F32),
            pltpu.VMEM((rows, 128), F32),
            pltpu.VMEM((RING, 1, rows), F32),
            pltpu.VMEM((2, 7, 1, rows), F32),
            pltpu.VMEM((2, 7, 1, rows), F32),
            dma((4,)),
            dma((2, 7, 2)),
            dma((2, 7, 2)),
            dma((2, 7, 2)),
            dma((2, 7, 2)),
            dma((2, 7)),
            dma((2, 7)),
            dma((3,)),
            dma((3,)),
            dma((2,)),
            dma((2,)),
            dma((1,)),
            dma((1,)),
        ],
        compiler_params=pltpu.CompilerParams(
            collective_id=0, has_side_effects=True, vmem_limit_bytes=48 * 2**20
        ),
        cost_estimate=pl.CostEstimate(
            flops=3 * 2 * 1024 * 512 * width, bytes_accessed=6 * rows * width, transcendentals=0
        ),
    )(image_embed, text_embed, both)
    return pl.pallas_call(
        write_out,
        out_shape=(
            jax.ShapeDtypeStruct((rows,), F32),
            jax.ShapeDtypeStruct((rows, width), F32),
            jax.ShapeDtypeStruct((rows, width), F32),
        ),
        in_specs=[vmem] * 7,
        out_specs=(anywhere, anywhere, anywhere),
        scratch_shapes=[pltpu.VMEM((rows,), F32), pltpu.VMEM((2, rows // 4, width), F32), dma((6,))],
        compiler_params=pltpu.CompilerParams(vmem_limit_bytes=4 * 2**20),
        cost_estimate=pl.CostEstimate(flops=0, bytes_accessed=16 * rows * width, transcendentals=0),
    )(*results, both)


def solution(mesh):
    placed = (P(("group", "blk"), None), P(("group", "blk"), None), P(), P())
    return jax.shard_map(
        per_device,
        mesh=mesh,
        in_specs=placed,
        out_specs=(P(("group", "blk")), P(("group", "blk"), None), P(("group", "blk"), None)),
        check_vma=False,
    )
```

profile of v0, /device:TPU:2, one launch (start us, length us, event | category | flops | bytes accessed | tf_op | source)
XLA Modules:
  0.0 56.8 jit_solution(13468822784937160217)
XLA Ops:
  1.9 0.1 iota.7.both_ref.both
  2.0 53.7 %shard_map.67 = (f32[1,128]{1,0:T(1,128)S(1)}, f32[128,1152]{1,0:T(8,128)S(1)}, f32[128,1152]{1,0:T(8,128)S(1)}, bf16[2,32,1152]{2,1,0:T(8,128)(2,1)S(1)}, f32[1...) custom-call(bf16[128,1152]{1,0:T(8,128)(2,1)} %img_hbm.1, bf16[128,1152]{1,0:T(8,128)(2,1)} %txt_hbm.1, ...), custom_call_target="tpu_custom_call" | custom-call | flops 3623878656 | bytes 884736 | tf_op jit(solution)/shard_map/pallas_call | solution.py:473
  55.7 1.1 %shard_map.68 = (f32[128]{0:T(128)}, f32[128,1152]{1,0:T(8,128)}, f32[128,1152]{1,0:T(8,128)}) custom-call(f32[1,128]{1,0:T(1,128)S(1)} %get-tuple-element.9.loss_in, f32[128,1152]{1,0:T(8,128)S(1)} %get-tuple-element.10.gi_in, f32[128,1152]{1,0:T(8,128)S(1)} %get-tuple-element.11.gt_in, bf16[2,32,1152]{2,1,0:T(8,128)(2,1)S(1)} %get-tuple-element.12.late, ...), custom_call_target="tpu_custom_call" | custom-call | bytes 2359296 | tf_op jit(solution)/shard_map/pallas_call | solution.py:524
  (1 shorter events, 0.0 us)
where the time goes:
time: 56.9 us; the launch traced here: 56.8 us
  Pallas kernels  54.7 us (96%)
  between operations  1.94 us (3%)
    pallas_call x1, Pallas kernels, per_device(): pl.pallas_call(kernel, out_shape=(pltpu.VMEM((1, rows), F32), pltpu.VMEM(...  53.7 us

commit v1 on v0

--- a/solution.py
+++ b/solution.py
@@ -137,7 +137,7 @@
         else:
             src = img.at[i - 1, pl.ds(place(way, i - 2, s), sub), :]
         dst = img.at[i + 1, pl.ds(place(way, i, s), sub), :]
-        return copy(src, dst, ag_ssem.at[way, i, s], ag_rsem.at[way, i, s], to[way])
+        return copy(src, dst, ag_ssem.at[0], ag_rsem.at[way, i, s], to[way])
 
     for i in range(2):
         load(i).wait()
@@ -211,7 +211,7 @@
     def gather_wait(way, i, s):
         row = pl.multiple_of(place(way, i, s), sub)
         some = img.at[i + 1, pl.ds(row, sub), :]
-        copy(some, some, ag_ssem.at[way, i, s], ag_rsem.at[way, i, s], to[way]).wait_recv()
+        copy(some, some, ag_ssem.at[0], ag_rsem.at[way, i, s], to[way]).wait_recv()
 
     def block_of(kind, j):
         return (7, 6, 4, 2)[j] if kind == LATE else (5, 3, 1)[j]
@@ -223,7 +223,7 @@
         return copy(
             rs_send.at[way, at, some, :],
             late_ref.at[way] if very_last else rs_recv.at[way, at, some, :],
-            rs_ssem.at[way, at, s],
+            rs_ssem.at[0],
             rs_rsem.at[way, at, s],
             to[way],
         )
@@ -252,7 +252,7 @@
         return copy(
             loss_send.at[way, at],
             loss_recv.at[way, at],
-            loss_ssem.at[way, at],
+            loss_ssem.at[0],
             loss_rsem.at[way, at],
             to[way],
         )
@@ -358,30 +358,6 @@
     loss_on(LATE, 3)
     pass_on(LATE, 3)
 
-    def sent(i, _):
-        for way in (RIGHT, LEFT):
-            for s in range(2):
-                some = img.at[i, pl.ds(s * sub, sub), :]
-                copy(some, some, ag_ssem.at[way, i, s], ag_rsem.at[way, i, s], to[way]).wait_send()
-        return 0
-
-    lax.fori_loop(0, 7, sent, 0)
-    for i in range(3):
-        text_copy(i).wait_send()
-    for i in range(2):
-        core_copy(i).wait_send()
-
-    def summed(at):
-        for way in (RIGHT, LEFT):
-            for s in range(2):
-                some = rs_send.at[way, at, pl.ds(s * sub, sub), :]
-                copy(some, some, rs_ssem.at[way, at, s], rs_rsem.at[way, at, s], to[way]).wait_send()
-            x = loss_send.at[way, at]
-            copy(x, x, loss_ssem.at[way, at], loss_rsem.at[way, at], to[way]).wait_send()
-
-    lax.fori_loop(0, 3, lambda i, _: (summed(i), 0)[1], 0)
-    lax.fori_loop(4, 7, lambda i, _: (summed(i), 0)[1], 0)
-
     def own_rows(way, kind, s):
         at = (half if (way == RIGHT) == (kind == EARLY) else 0) + s * sub
         return pl.ds(pl.multiple_of(at, sub), sub)
@@ -420,6 +396,14 @@
         + jnp.concatenate(lanes(RIGHT, LATE) + lanes(RIGHT, EARLY), axis=1)
         + jnp.concatenate(lanes(LEFT, EARLY) + lanes(LEFT, LATE), axis=1)
     )
+    def all_sent(x, ssem, rsem):
+        copy(x, x, ssem, rsem, to[RIGHT]).wait_send()
+
+    all_sent(img.at[pl.ds(0, 7)], ag_ssem.at[0], ag_rsem.at[0, 0, 0])
+    for i in range(3):
+        text_copy(i).wait_send()
+    for i in range(2):
+        core_copy(i).wait_send()
     y_copy.wait_send()
 
     for way in (RIGHT, LEFT):
@@ -430,7 +414,8 @@
         gi_ref[at, :] = unnormal(g, unit_i[at, :], inv_i[at, :], scale)
     for way in (RIGHT, LEFT):
         chunk(way, LATE, 3, 1).wait_recv()
-    summed(3)
+    all_sent(rs_send, rs_ssem.at[0], rs_rsem.at[0, 0, 0])
+    all_sent(loss_send, loss_ssem.at[0], loss_rsem.at[0, 0])
 
 
 def write_out(
@@ -501,11 +486,11 @@
             pltpu.VMEM((2, 7, 1, rows), F32),
             pltpu.VMEM((2, 7, 1, rows), F32),
             dma((4,)),
+            dma((1,)),
             dma((2, 7, 2)),
+            dma((1,)),
             dma((2, 7, 2)),
-            dma((2, 7, 2)),
-            dma((2, 7, 2)),
-            dma((2, 7)),
+            dma((1,)),
             dma((2, 7)),
             dma((3,)),
             dma((3,)),

time: 56.9 us -> 56.3 us (0.989)
  Pallas kernels: 54.7 us -> 54.1 us
    pallas_call x1, Pallas kernels: 53.7 us -> 53.1 us  [per_device(): pl.pallas_call(kernel, out_shape=(pltpu.VMEM((1, rows), F32), pltpu.VMEM(...]
where the time goes in v1:
time: 56.3 us; the launch traced here: 56.1 us
  Pallas kernels  54.1 us (96%)
  between operations  1.94 us (3%)
    pallas_call x1, Pallas kernels, per_device(): pl.pallas_call(kernel, out_shape=(pltpu.VMEM((1, rows), F32), pltpu.VMEM(...  53.1 us

profile of v1, /device:TPU:2, one launch (start us, length us, event | category | flops | bytes accessed | tf_op | source)
XLA Modules:
  0.0 56.1 jit_solution(15450785929157123594)
XLA Ops:
  1.9 0.1 iota.7.both_ref.both
  2.0 53.1 %shard_map.67 = (f32[1,128]{1,0:T(1,128)S(1)}, f32[128,1152]{1,0:T(8,128)S(1)}, f32[128,1152]{1,0:T(8,128)S(1)}, bf16[2,32,1152]{2,1,0:T(8,128)(2,1)S(1)}, f32[1...) custom-call(bf16[128,1152]{1,0:T(8,128)(2,1)} %img_hbm.1, bf16[128,1152]{1,0:T(8,128)(2,1)} %txt_hbm.1, ...), custom_call_target="tpu_custom_call" | custom-call | flops 3623878656 | bytes 884736 | tf_op jit(solution)/shard_map/pallas_call | solution.py:458
  55.1 1.1 %shard_map.68 = (f32[128]{0:T(128)}, f32[128,1152]{1,0:T(8,128)}, f32[128,1152]{1,0:T(8,128)}) custom-call(f32[1,128]{1,0:T(1,128)S(1)} %get-tuple-element.9.loss_in, f32[128,1152]{1,0:T(8,128)S(1)} %get-tuple-element.10.gi_in, f32[128,1152]{1,0:T(8,128)S(1)} %get-tuple-element.11.gt_in, bf16[2,32,1152]{2,1,0:T(8,128)(2,1)S(1)} %get-tuple-element.12.late, ...), custom_call_target="tpu_custom_call" | custom-call | bytes 2359296 | tf_op jit(solution)/shard_map/pallas_call | solution.py:509
  (1 shorter events, 0.0 us)

commit v2 on v1

--- a/solution.py
+++ b/solution.py
@@ -155,7 +155,7 @@
         normalize(txt_ref, i * half, half, unit_t, inv_t, txt)
 
     scale = both_ref[0:1, 0:1]
-    bias = both_ref[1:2, 0:1]
+    bias = both_ref[0:1, 1:2]
 
     def text_copy(i):
         src = (0, 0, 2)[i]
@@ -216,9 +216,15 @@
     def block_of(kind, j):
         return (7, 6, 4, 2)[j] if kind == LATE else (5, 3, 1)[j]
 
+    def whole(kind, j):
+        return kind == EARLY and j < 2
+
     def chunk(way, kind, j, s):
         at = 4 * kind + j
-        some = pl.ds(pl.multiple_of(s * sub, sub), sub)
+        if whole(kind, j):
+            some, s = pl.ds(0, half), 0
+        else:
+            some = pl.ds(pl.multiple_of(s * sub, sub), sub)
         very_last = kind == LATE and j == 3 and s == 1
         return copy(
             rs_send.at[way, at, some, :],
@@ -228,43 +234,56 @@
             to[way],
         )
 
+    def add_to(way, kind, j, s):
+        some = pl.ds(pl.multiple_of(s * sub, sub), sub)
+        row = pl.multiple_of(s * half + (1 - way) * sub, sub)
+        x = part[block_of(kind, j), pl.ds(row, sub), :]
+        if j > 0:
+            x = x + decode(rs_recv[way, 4 * kind + j - 1, some, :])
+        rs_send[way, 4 * kind + j, some, :] = encode(x)
+
     def pass_on(kind, j, first=0, count=2):
         def one(s, _):
-            some = pl.ds(pl.multiple_of(s * sub, sub), sub)
             for way in (RIGHT, LEFT):
-                row = pl.multiple_of(s * half + (1 - way) * sub, sub)
-                x = part[block_of(kind, j), pl.ds(row, sub), :]
-                if j > 0:
+                if j > 0 and not (whole(kind, j - 1) and first > 0):
                     chunk(way, kind, j - 1, s).wait_recv()
-                    x = x + decode(rs_recv[way, 4 * kind + j - 1, some, :])
-                rs_send[way, 4 * kind + j, some, :] = encode(x)
+                add_to(way, kind, j, s)
                 chunk(way, kind, j, s).start()
             return 0
 
-        if j == 3:
+        if whole(kind, j):
+            for way in (RIGHT, LEFT):
+                if j > 0:
+                    chunk(way, kind, j - 1, 0).wait_recv()
+                for s in range(2):
+                    add_to(way, kind, j, s)
+                chunk(way, kind, j, 0).start()
+        elif j == 3:
             one(0, 0)
             one(1, 0)
         else:
             lax.fori_loop(first, first + count, one, 0)
 
-    def loss_copy(way, kind, j):
-        at = 4 * kind + j
+    def loss_copy(way, j):
         return copy(
-            loss_send.at[way, at],
-            loss_recv.at[way, at],
+            loss_send.at[way, j],
+            loss_recv.at[way, j],
             loss_ssem.at[0],
-            loss_rsem.at[way, at],
+            loss_rsem.at[way, j],
             to[way],
         )
 
-    def loss_on(kind, j):
+    def loss_on(j):
         for way in (RIGHT, LEFT):
-            x = loss_part[block_of(kind, j)]
+            late = loss_part[block_of(LATE, j)]
+            early = jnp.zeros_like(late)
             if j > 0:
-                loss_copy(way, kind, j - 1).wait_recv()
-                x = x + loss_recv[way, 4 * kind + j - 1]
-            loss_send[way, 4 * kind + j] = x
-            loss_copy(way, kind, j).start()
+                loss_copy(way, j - 1).wait_recv()
+                late = late + loss_recv[way, j - 1, 0:1, :]
+                early = loss_part[block_of(EARLY, j - 1)] + loss_recv[way, j - 1, 1:2, :]
+            loss_send[way, j, 0:1, :] = late
+            loss_send[way, j, 1:2, :] = early
+            loss_copy(way, j).start()
 
     for i in range(2):
         serve(i, 0)
@@ -292,7 +311,6 @@
 
         @pl.when(k == 5)
         def _():
-            loss_on(EARLY, 0)
             pass_on(EARLY, 0)
 
         @pl.when(k == 6)
@@ -309,7 +327,7 @@
         for way in (RIGHT, LEFT):
             gather_wait(way, 6, s)
         tile(7, pl.multiple_of(s * half, half), half)
-        pl.when(s == 1)(lambda: loss_on(LATE, 0))
+        pl.when(s == 1)(lambda: loss_on(0))
         pass_on(LATE, 0, s, 1)
         return 0
 
@@ -337,25 +355,23 @@
         @pl.when(k == 1)
         def _():
             core_copy(0).start()
-            loss_on(EARLY, 1)
             pass_on(EARLY, 1)
 
         return 0
 
     lax.fori_loop(0, QUAD, sums_work, 0)
-    loss_on(LATE, 1)
+    loss_on(1)
     pass_on(LATE, 1)
     core_copy(1).wait_recv()
     y_send[...] = encode(sums[2] + core_recv[1])
     y_copy.start()
-    loss_on(EARLY, 2)
     pass_on(EARLY, 2, 0, 1)
-    loss_on(LATE, 2)
+    loss_on(2)
     pass_on(LATE, 2)
     pass_on(EARLY, 2, 1, 1)
     core_copy(0).wait_recv()
     sums[0] += core_recv[0]
-    loss_on(LATE, 3)
+    loss_on(3)
     pass_on(LATE, 3)
 
     def own_rows(way, kind, s):
@@ -386,11 +402,12 @@
     lax.fori_loop(0, 4, finish_text, 0)
 
     def lanes(way, kind):
-        loss_copy(way, kind, 3 - kind).wait_recv()
-        x = loss_recv[way, 4 * kind + 3 - kind]
+        x = loss_recv[way, 3, kind : kind + 1, :]
         at = (1 - way) * sub
         return [x[:, s * half + at : s * half + at + sub] for s in range(2)]
 
+    for way in (RIGHT, LEFT):
+        loss_copy(way, 3).wait_recv()
     loss_ref[...] = (
         loss_part[0]
         + jnp.concatenate(lanes(RIGHT, LATE) + lanes(RIGHT, EARLY), axis=1)
@@ -452,8 +469,8 @@
     hbm = pl.BlockSpec(memory_space=pltpu.HBM)
     image_embed = pltpu.with_memory_space_constraint(image_embed, pltpu.HBM)
     text_embed = pltpu.with_memory_space_constraint(text_embed, pltpu.HBM)
-    row = lax.broadcasted_iota(jnp.int32, (8, 128), 0)
-    both = jnp.where(row == 0, logit_scale[0], logit_bias[0])
+    lane = lax.broadcasted_iota(jnp.int32, (1, 128), 1)
+    both = jnp.where(lane == 0, logit_scale[0], logit_bias[0])
     anywhere = pl.BlockSpec(memory_space=pl.ANY)
     results = pl.pallas_call(
         kernel,
@@ -483,15 +500,15 @@
             pltpu.VMEM((rows, width), F32),
             pltpu.VMEM((rows, 128), F32),
             pltpu.VMEM((RING, 1, rows), F32),
-            pltpu.VMEM((2, 7, 1, rows), F32),
-            pltpu.VMEM((2, 7, 1, rows), F32),
+            pltpu.VMEM((2, 4, 2, rows), F32),
+            pltpu.VMEM((2, 4, 2, rows), F32),
             dma((4,)),
             dma((1,)),
             dma((2, 7, 2)),
             dma((1,)),
             dma((2, 7, 2)),
             dma((1,)),
-            dma((2, 7)),
+            dma((2, 4)),
             dma((3,)),
             dma((3,)),
             dma((2,)),

time: 56.3 us -> 56.2 us (level)
  no operation moved by 1% of the time
where the time goes in v2:
time: 56.2 us; the launch traced here: 56.1 us
  Pallas kernels  54.2 us (96%)
  between operations  1.94 us (3%)
    pallas_call x1, Pallas kernels, per_device(): pl.pallas_call(kernel, out_shape=(pltpu.VMEM((1, rows), F32), pltpu.VMEM(...  53.1 us

profile of v2, /device:TPU:2, one launch (start us, length us, event | category | flops | bytes accessed | tf_op | source)
XLA Modules:
  0.0 56.1 jit_solution(17462702262698062668)
XLA Ops:
  1.9 53.1 %shard_map.67 = (f32[1,128]{1,0:T(1,128)S(1)}, f32[128,1152]{1,0:T(8,128)S(1)}, f32[128,1152]{1,0:T(8,128)S(1)}, bf16[2,32,1152]{2,1,0:T(8,128)(2,1)S(1)}, f32[1...) custom-call(bf16[128,1152]{1,0:T(8,128)(2,1)} %img_hbm.1, bf16[128,1152]{1,0:T(8,128)(2,1)} %txt_hbm.1, ...), custom_call_target="tpu_custom_call" | custom-call | flops 3623878656 | bytes 884736 | tf_op jit(solution)/shard_map/pallas_call | solution.py:475
  55.0 1.1 %shard_map.68 = (f32[128]{0:T(128)}, f32[128,1152]{1,0:T(8,128)}, f32[128,1152]{1,0:T(8,128)}) custom-call(f32[1,128]{1,0:T(1,128)S(1)} %get-tuple-element.9.loss_in, f32[128,1152]{1,0:T(8,128)S(1)} %get-tuple-element.10.gi_in, f32[128,1152]{1,0:T(8,128)S(1)} %get-tuple-element.11.gt_in, bf16[2,32,1152]{2,1,0:T(8,128)(2,1)S(1)} %get-tuple-element.12.late, ...), custom_call_target="tpu_custom_call" | custom-call | bytes 2359296 | tf_op jit(solution)/shard_map/pallas_call | solution.py:526
  (1 shorter events, 0.0 us)

commit v3 on v1

--- a/solution.py
+++ b/solution.py
@@ -155,7 +155,7 @@
         normalize(txt_ref, i * half, half, unit_t, inv_t, txt)
 
     scale = both_ref[0:1, 0:1]
-    bias = both_ref[1:2, 0:1]
+    bias = both_ref[0:1, 1:2]
 
     def text_copy(i):
         src = (0, 0, 2)[i]
@@ -338,13 +338,14 @@
         def _():
             core_copy(0).start()
             loss_on(EARLY, 1)
-            pass_on(EARLY, 1)
+            pass_on(EARLY, 1, 0, 1)
 
         return 0
 
     lax.fori_loop(0, QUAD, sums_work, 0)
     loss_on(LATE, 1)
     pass_on(LATE, 1)
+    pass_on(EARLY, 1, 1, 1)
     core_copy(1).wait_recv()
     y_send[...] = encode(sums[2] + core_recv[1])
     y_copy.start()
@@ -452,8 +453,8 @@
     hbm = pl.BlockSpec(memory_space=pltpu.HBM)
     image_embed = pltpu.with_memory_space_constraint(image_embed, pltpu.HBM)
     text_embed = pltpu.with_memory_space_constraint(text_embed, pltpu.HBM)
-    row = lax.broadcasted_iota(jnp.int32, (8, 128), 0)
-    both = jnp.where(row == 0, logit_scale[0], logit_bias[0])
+    lane = lax.broadcasted_iota(jnp.int32, (1, 128), 1)
+    both = jnp.where(lane == 0, logit_scale[0], logit_bias[0])
     anywhere = pl.BlockSpec(memory_space=pl.ANY)
     results = pl.pallas_call(
         kernel,

time: 56.3 us -> 56.3 us (level)
  no operation moved by 1% of the time
where the time goes in v3:
time: 56.3 us; the launch traced here: 56.1 us
  Pallas kernels  54.2 us (96%)
  between operations  1.94 us (3%)
    pallas_call x1, Pallas kernels, per_device(): pl.pallas_call(kernel, out_shape=(pltpu.VMEM((1, rows), F32), pltpu.VMEM(...  53.1 us

profile of v3, /device:TPU:2, one launch (start us, length us, event | category | flops | bytes accessed | tf_op | source)
XLA Modules:
  0.0 56.1 jit_solution(5746596637396725368)
XLA Ops:
  1.9 53.1 %shard_map.67 = (f32[1,128]{1,0:T(1,128)S(1)}, f32[128,1152]{1,0:T(8,128)S(1)}, f32[128,1152]{1,0:T(8,128)S(1)}, bf16[2,32,1152]{2,1,0:T(8,128)(2,1)S(1)}, f32[1...) custom-call(bf16[128,1152]{1,0:T(8,128)(2,1)} %img_hbm.1, bf16[128,1152]{1,0:T(8,128)(2,1)} %txt_hbm.1, ...), custom_call_target="tpu_custom_call" | custom-call | flops 3623878656 | bytes 884736 | tf_op jit(solution)/shard_map/pallas_call | solution.py:459
  55.1 1.1 %shard_map.68 = (f32[128]{0:T(128)}, f32[128,1152]{1,0:T(8,128)}, f32[128,1152]{1,0:T(8,128)}) custom-call(f32[1,128]{1,0:T(1,128)S(1)} %get-tuple-element.9.loss_in, f32[128,1152]{1,0:T(8,128)S(1)} %get-tuple-element.10.gi_in, f32[128,1152]{1,0:T(8,128)S(1)} %get-tuple-element.11.gt_in, bf16[2,32,1152]{2,1,0:T(8,128)(2,1)S(1)} %get-tuple-element.12.late, ...), custom_call_target="tpu_custom_call" | custom-call | bytes 2359296 | tf_op jit(solution)/shard_map/pallas_call | solution.py:510
  (1 shorter events, 0.0 us)
